TPU v7x, 256 devices: a whole 4x4x8 slice. The times are simulated.
256 devices in a mesh: ctx: 32 (over z, x), kvh: 8 (over y, core).
Axes of the slice: x: 4, y: 4, z: 8, core: 2. Of those that a mesh axis runs over, the one named last changes fastest.
Arguments:
- queries: bfloat16 [8, 2048, 1024], P('kvh', 'ctx'), may hold values from -15 to 15
- span_kv: bfloat16 [2, 8, 2048, 128], P(None, 'kvh', 'ctx'), may hold values from -6 to 6
- cache_kv: bfloat16 [2, 8, 262144, 128], P(None, 'kvh', 'ctx'), may hold values from -6 to 6
- choices: int32 [8, 2048, 3], P('kvh'), may hold values from 0 to 63, all different within a row; in each aligned block of 64 rows (0 to 63, 64 to 127, ..., all dimensions but the last counted through in order) at most 4 rows name the same one
- block_home: int32 [64], replicated, may hold values from 0 to 63, each once
- out_weight: bfloat16 [8192, 4096], P('kvh'), may hold values from -0.0625 to 0.0625
Outputs:
- attended: bfloat16 [8, 2048, 1024], P('kvh', 'ctx')
- projected: bfloat16 [2048, 4096], P(('ctx', 'kvh'))
Inputs may be any that keep to these rules, and one draw needn't show every extreme that they name: `choices`: each row names 3 different blocks. Among the rows k * 64 to (k + 1) * 64 - 1 of one KV head, at most 4 rows name the same block. `block_home`: each storage slot holds exactly one block.
All inputs are finite; a program needn't handle non-finite values.
Results may differ from a plain program's by a relative error of at most 0.019.
Values may be sent and summed in bfloat16 or wider, within the bound.
A program may use at most 128 MiB of HBM per device.

v0:
```python
import math

import jax
import jax.numpy as jnp
from jax import lax
from jax.sharding import PartitionSpec as P


def block_attention(query_rows, key_rows, value_rows, score_scale, allowed):
    scores = (
        lax.dot_general(
            query_rows, key_rows, (((1,), (1,)), ((), ())), preferred_element_type=jnp.float32
        )
        * score_scale
    )
    if allowed is not None:
        scores = jnp.where(allowed, scores, -1e30)
    peak_value = jnp.max(scores, axis=1, keepdims=True)
    exponent = jnp.exp(scores - peak_value)
    totals = jnp.sum(exponent, axis=1, keepdims=True)
    weights = exponent.astype(jnp.bfloat16)
    part_out = jnp.dot(weights, value_rows, preferred_element_type=jnp.float32) / totals
    return (part_out, (peak_value + jnp.log(totals))[:, 0])


def merge_parts(own_out, own_lse, far_out, far_lse):
    all_lse = jnp.concatenate([own_lse[:, None], far_lse], axis=1)
    all_out = jnp.concatenate([own_out[:, None], far_out.astype(jnp.float32)], axis=1)
    peak_value = jnp.max(all_lse, axis=1, keepdims=True)
    factors = jnp.exp(all_lse - peak_value)
    return jnp.sum(factors[..., None] * all_out, axis=1) / jnp.sum(factors, axis=1)[..., None]


def slot_numbers(picks, block_home, slot_cap):
    pair_count = picks.shape[1]
    block_count = block_home.shape[0]
    pair_ids = jnp.arange(pair_count, dtype=jnp.int32)
    same_block = picks[:, :, None] == picks[:, None, :]
    earlier = pair_ids[None, :] < pair_ids[:, None]
    rank_in = jnp.sum(jnp.logical_and(same_block, earlier[None]), axis=2)
    matches = picks[:, :, None] == jnp.arange(block_count, dtype=jnp.int32)[None, None, :]
    storage = jnp.sum(jnp.where(matches, block_home[None, None, :], 0), axis=2)
    return (storage, storage * slot_cap + rank_in)


def on_device(queries, span_kv, cache_kv, choices, block_home, out_weight):
    n_ctx = lax.axis_size("ctx")
    my_index = lax.axis_index("ctx")
    q_dev = queries.shape[1]
    row_width = queries.shape[2]
    head_dim = cache_kv.shape[3]
    group_size = row_width // head_dim
    top_count = choices.shape[2]
    block_count = block_home.shape[0]
    blk_dev = block_count // n_ctx
    block_len = cache_kv.shape[2] // blk_dev
    slot_cap = max(2, (4 * q_dev * top_count + 3 * block_count - 1) // (3 * block_count))
    slot_count = block_count * slot_cap
    score_scale = 1.0 / math.sqrt(head_dim)
    cache_keys = cache_kv[0, 0].reshape(blk_dev, block_len, head_dim)
    cache_values = cache_kv[1, 0].reshape(blk_dev, block_len, head_dim)
    slot_ids = jnp.arange(slot_count, dtype=jnp.int32)
    my_picks = lax.dynamic_slice_in_dim(choices[0], my_index * q_dev, q_dev, 0).reshape(
        1, q_dev * top_count
    )
    my_home, my_place = slot_numbers(my_picks, block_home, slot_cap)
    every_query = lax.all_gather(queries, "ctx", axis=1, tiled=True)
    all_home, all_place = slot_numbers(
        choices[0].reshape(n_ctx, q_dev * top_count), block_home, slot_cap
    )
    source = jnp.arange(n_ctx, dtype=jnp.int32)[:, None]
    local_slot = (source * blk_dev + all_home % blk_dev) * slot_cap + all_place % slot_cap
    local_slot = jnp.where(all_home // blk_dev == my_index, local_slot, -1)
    selector = jnp.any(
        local_slot.reshape(n_ctx * q_dev, top_count)[:, :, None] == slot_ids[None, None, :], axis=1
    ).astype(jnp.bfloat16)
    incoming = lax.dot_general(
        selector, every_query[0], (((0,), (0,)), ((), ())), preferred_element_type=jnp.float32
    ).astype(jnp.bfloat16)
    received = incoming.reshape(n_ctx, blk_dev, slot_cap, row_width)
    item_count = received.shape[2]

    def one_block(element):
        block_rows, key_rows, value_rows = element
        part_out, part_lse = block_attention(
            block_rows.reshape(n_ctx * item_count * group_size, head_dim),
            key_rows,
            value_rows,
            score_scale,
            None,
        )
        return (
            part_out.astype(jnp.bfloat16).reshape(n_ctx, item_count, row_width),
            part_lse.reshape(n_ctx, item_count, group_size),
        )

    block_outs, block_lses = lax.map(
        one_block, (jnp.moveaxis(received, 1, 0), cache_keys, cache_values)
    )
    sent_out = lax.all_to_all(
        jnp.moveaxis(block_outs, 0, 1), "ctx", split_axis=0, concat_axis=0, tiled=True
    )
    sent_lse = lax.all_to_all(
        jnp.moveaxis(block_lses, 0, 1), "ctx", split_axis=0, concat_axis=0, tiled=True
    )
    far_out = jnp.take(sent_out.reshape(slot_count, row_width), my_place[0], axis=0).reshape(
        q_dev, top_count, group_size, head_dim
    )
    far_lse = jnp.take(sent_lse.reshape(slot_count, group_size), my_place[0], axis=0).reshape(
        q_dev, top_count, group_size
    )
    span_all = lax.all_gather(span_kv, "ctx", axis=2, tiled=True)
    q_rows = queries[0].reshape(q_dev * group_size, head_dim)
    row_pos = jnp.repeat(my_index * q_dev + jnp.arange(q_dev, dtype=jnp.int32), group_size)
    key_pos = jnp.arange(span_all.shape[2], dtype=jnp.int32)
    allowed = key_pos[None, :] <= row_pos[:, None]
    own_out, own_lse = block_attention(q_rows, span_all[0, 0], span_all[1, 0], score_scale, allowed)
    combined = merge_parts(
        own_out.reshape(q_dev, group_size, head_dim),
        own_lse.reshape(q_dev, group_size),
        far_out,
        far_lse,
    )
    attended = combined.reshape(q_dev, row_width).astype(jnp.bfloat16)
    projected = lax.psum_scatter(
        jnp.dot(attended, out_weight, preferred_element_type=jnp.float32).astype(jnp.bfloat16),
        "kvh",
        scatter_dimension=0,
        tiled=True,
    )
    return (attended[None], projected)


def solution(mesh):
    return jax.shard_map(
        on_device,
        mesh=mesh,
        in_specs=(
            P("kvh", "ctx", None),
            P(None, "kvh", "ctx", None),
            P(None, "kvh", "ctx", None),
            P("kvh", None, None),
            P(),
            P("kvh", None),
        ),
        out_specs=(P("kvh", "ctx", None), P(("ctx", "kvh"), None)),
        check_vma=False,
    )
```

profile of v0, /device:TPU:1, one launch (start us, length us, event | category | flops | bytes accessed | tf_op | source)
XLA Modules:
  0.0 309.0 jit_solution(5779730361639696033)
XLA Ops:
  8.7 1.0 reshape_squeeze.9
  9.6 1.1 copy.41
  11.2 1.2 select_reduce_fusion
  12.4 1.0 reduce_sum.80
  13.4 2.4 convert_reduce_fusion
  15.9 1.0 reduce_sum.82
  17.0 1.5 fusion.43
  20.5 1.4 fusion.22
  22.0 3.8 %fusion.55 = (bf16[1,1,8192,128]{3,2,1,0:T(8,128)(2,1)}, bf16[1,1,8192,128]{3,2,1,0:T(8,128)(2,1)S(1)}) fusion(bf16[2,1,8192,128]{3,2,1,0:T(8,128)(2,1)} %param.10), kind=kLoop, calls=%fused_computation.85 | loop fusion | bytes 8388608 | tf_op jit(solution)/shard_map/slice | solution.py:61
  25.8 60.3 %all-gather.3.cloned.1.call-done = bf16[2,1,2048,128]{3,2,1,0:T(8,128)(2,1)} async-done(((bf16[2,1,64,128]{3,2,1,0:T(8,128)(2,1)}), bf16[2,1,2048,128]{3,2,1,0:T(8,128)(2,1)}) %all-gather.3.cloned.1.call-update) | async-done | bytes 1048592 | tf_op jit(solution)/shard_map/all_gather | solution.py:112
  86.2 3.8 %fusion.56 = (f32[512]{0:T(512)S(1)}, f32[512,2048]{1,0:T(8,128)}) fusion(bf16[512,128]{1,0:T(8,128)(2,1)S(1)} %reshape_squeeze.9, bf16[2,1,2048,128]{3,2,1,0:T(8,128)(2,1)} %all-gather.3.cloned.1.call-done, s32[512]{0:T(512)S(1)} %le.32), kind=kOutput, calls=%fused_computation.86 | convolution fusion | flops 272629248 | bytes 4853760 | tf_op jit(solution)/shard_map/dot_general | solution.py:11
  90.0 80.0 %all-gather.5.cloned.1.call-done = bf16[1,2048,1024]{2,1,0:T(8,128)(2,1)} async-done(((bf16[1,64,1024]{2,1,0:T(8,128)(2,1)}), bf16[1,2048,1024]{2,1,0:T(8,128)(2,1)}) %all-gather.5.cloned.1.call-update) | async-done | bytes 4194320 | tf_op jit(solution)/shard_map/all_gather | solution.py:67
  170.0 4.3 %fusion.30 = bf16[256,1024]{1,0:T(8,128)(2,1)} fusion(pred[2048,256]{1,0:T(8,128)(4,1)S(1)} %fusion.22, bf16[1,2048,1024]{2,1,0:T(8,128)(2,1)} %all-gather.5.cloned.1.call-done), kind=kOutput, calls=%fused_computation.44 | convolution fusion | flops 1074003968 | bytes 5242880 | tf_op jit(solution)/shard_map/dot_general | solution.py:77
  174.3 1.2 reshape.459
  175.7 54.7 %while.12 = (s32[]{:T(128)}, bf16[2,32,4,1024]{3,2,0,1:T(4,128)(2,1)}, f32[2,32,4,8]{3,2,0,1:T(4,128)}, bf16[2,32,4,1024]{3,2,1,0:T(4,128)(2,1)S(1)}, bf16[2,409...) while((s32[]{:T(128)}, bf16[2,32,4,1024]{3,2,0,1:T(4,128)(2,1)}, ...), condition=%wide.region_10.11_spmd, body=%wide.region_7.10_spmd.sunk | while | flops 2181299200 | bytes 55160936 | solution.py:97
  176.1 8.1 %multiply_reduce_fusion.2 = (f32[1024]{0:T(1024)S(1)}, f32[1024,4096]{1,0:T(8,128)}) fusion(bf16[1024,128]{1,0:T(8,128)(2,1)S(1)} %reshape.479, bf16[2,4096,128]{2,1,0:T(8,128)(2,1)S(1)} %get-tuple-element.118, s32[]{:T(128)S(6)} %copy.72), kind=kOutput, calls=%fused_computation.3.clone.1 | convolution fusion | flops 1082129408 | bytes 18092036 | tf_op jit(solution)/shard_map/while/body/eval_jaxpr/dot_general | solution.py:11
  184.2 8.6 %fusion.69 = f32[1024]{0:T(1024)S(1)} fusion(f32[1024,4096]{1,0:T(8,128)} %get-tuple-element.98, f32[1024]{0:T(1024)S(1)} %get-tuple-element.99), kind=kLoop, calls=%fused_computation.4.clone.1 | loop fusion | flops 12581888 | bytes 16785408 | tf_op jit(solution)/shard_map/while/body/eval_jaxpr/reduce_sum | solution.py:20
  192.8 8.7 %fusion.70 = bf16[1024,128]{1,0:T(8,128)(2,1)S(1)} fusion(bf16[2,4096,128]{2,1,0:T(8,128)(2,1)} %get-tuple-element.119, s32[]{:T(128)S(6)} %copy.72, f32[1024,4096]{1,0:T(8,128)} %get-tuple-element.98, f32[1024]{0:T(1024)S(1)} %get-tuple-element.99, f32[1024]{0:T(1024)S(1)} %fusion.69), kind=kOutput, calls=%fused_computation.13.clone.1 | convolution fusion | flops 1086586880 | bytes 18096132 | tf_op jit(solution)/shard_map/while/body/eval_jaxpr/dot_general | solution.py:22
  201.5 0.8 bitcast_dynamic-update-slice_fusion.4
  203.3 8.1 %multiply_reduce_fusion.2 = (f32[1024]{0:T(1024)S(1)}, f32[1024,4096]{1,0:T(8,128)}) fusion(bf16[1024,128]{1,0:T(8,128)(2,1)S(1)} %reshape.479, bf16[2,4096,128]{2,1,0:T(8,128)(2,1)S(1)} %get-tuple-element.118, s32[]{:T(128)S(6)} %copy.72), kind=kOutput, calls=%fused_computation.3.clone.1 | convolution fusion | flops 1082129408 | bytes 18092036 | tf_op jit(solution)/shard_map/while/body/eval_jaxpr/dot_general | solution.py:11
  211.4 8.6 %fusion.69 = f32[1024]{0:T(1024)S(1)} fusion(f32[1024,4096]{1,0:T(8,128)} %get-tuple-element.98, f32[1024]{0:T(1024)S(1)} %get-tuple-element.99), kind=kLoop, calls=%fused_computation.4.clone.1 | loop fusion | flops 12581888 | bytes 16785408 | tf_op jit(solution)/shard_map/while/body/eval_jaxpr/reduce_sum | solution.py:20
  220.0 8.7 %fusion.70 = bf16[1024,128]{1,0:T(8,128)(2,1)S(1)} fusion(bf16[2,4096,128]{2,1,0:T(8,128)(2,1)} %get-tuple-element.119, s32[]{:T(128)S(6)} %copy.72, f32[1024,4096]{1,0:T(8,128)} %get-tuple-element.98, f32[1024]{0:T(1024)S(1)} %get-tuple-element.99, f32[1024]{0:T(1024)S(1)} %fusion.69), kind=kOutput, calls=%fused_computation.13.clone.1 | convolution fusion | flops 1086586880 | bytes 18096132 | tf_op jit(solution)/shard_map/while/body/eval_jaxpr/dot_general | solution.py:22
  228.8 0.8 bitcast_dynamic-update-slice_fusion.4
  230.4 5.8 %all-to-all-start = ((f32[32,2,4,8]{3,2,1,0:T(4,128)}), f32[32,2,4,8]{3,2,1,0:T(4,128)S(1)}, u32[]{:S(2)}, u32[]{:S(2)}) async-start(f32[32,2,4,8]{3,2,1,0:T(4,128)} %bitcast.7), calls=%async_computation | async-start | bytes 262144 | tf_op jit(solution)/shard_map/all_to_all | solution.py:103
  236.2 2.9 fusion.26
  239.0 6.5 %all-to-all-done = f32[32,2,4,8]{3,2,1,0:T(4,128)S(1)} async-done(((f32[32,2,4,8]{3,2,1,0:T(4,128)}), f32[32,2,4,8]{3,2,1,0:T(4,128)S(1)}, u32[]{:S(2)}, u32[]{:S(2)}) %all-to-all-start) | async-done | bytes 8224 | tf_op jit(solution)/shard_map/all_to_all | solution.py:103
  245.5 3.9 %all-to-all-start.1 = ((bf16[32,2,4,1024]{3,2,1,0:T(4,128)(2,1)}), bf16[32,2,4,1024]{3,2,1,0:T(4,128)(2,1)S(1)}, u32[]{:S(2)}, u32[]{:S(2)}) async-start(bf16[32,2,4,1024]{3,2,1,0:T(4,128)(2,1)} %bitcast.14), calls=%async_computation.1 | async-start | bytes 1048576 | tf_op jit(solution)/shard_map/all_to_all | solution.py:100
  249.9 3.0 fusion.36
  254.2 8.1 %all-to-all-done.1 = bf16[32,2,4,1024]{3,2,1,0:T(4,128)(2,1)S(1)} async-done(((bf16[32,2,4,1024]{3,2,1,0:T(4,128)(2,1)}), bf16[32,2,4,1024]{3,2,1,0:T(4,128)(2,1)S(1)}, u32[]{:S(2)}, u32[]{:S(2)}) %all-to-all-start.1) | async-done | bytes 524320 | tf_op jit(solution)/shard_map/all_to_all | solution.py:100
  262.5 1.0 gather_fusion.1
  264.4 5.7 %convolution_convert_fusion = bf16[64,4096]{1,0:T(8,128)(2,1)} fusion(bf16[1024,4096]{1,0:T(8,128)(2,1)} %param.13, bf16[8,8,8,128]{3,2,1,0:T(8,128)(2,1)S(1)} %bitcast.68), kind=kOutput, calls=%fused_computation.24 | convolution fusion | flops 537133056 | bytes 9043968 | tf_op jit(solution)/shard_map/dot_general | solution.py:126
  270.8 31.6 %reduce-scatter.2.cloned.1.call-done = bf16[8,4096]{1,0:T(8,128)(2,1)} async-done(((bf16[64,4096]{1,0:T(8,128)(2,1)}), bf16[8,4096]{1,0:T(8,128)(2,1)}) %reduce-scatter.2.cloned.1.call-update) | async-done | bytes 65552 | tf_op jit(solution)/shard_map/reduce_scatter | solution.py:125
  (63 shorter events, 9.7 us)
Async XLA Ops:
  7.2 79.0 %all-gather.3.cloned.1.call-start = ((), (), s32[]{:S(2)}) async-start(), calls=%async_computation.3 | async-start | bytes 1081344 | tf_op jit(solution)/shard_map/all_gather | solution.py:112
  7.9 162.1 %all-gather.5.cloned.1.call-start = ((), (), s32[]{:S(2)}) async-start(), calls=%async_computation.4 | async-start | bytes 4325376 | tf_op jit(solution)/shard_map/all_gather | solution.py:67
  10.7 9.2 %copy-start.1 = (s32[64]{0:T(128)S(1)}, s32[64]{0:T(128)}, u32[]{:S(2)}) copy-start(s32[64]{0:T(128)} %param.12) | copy-start | bytes 772
  230.4 19.6 %copy-start = (bf16[2,1,2048,128]{3,2,1,0:T(8,128)(2,1)S(1)}, bf16[2,1,2048,128]{3,2,1,0:T(8,128)(2,1)}, u32[]{:S(2)}) copy-start(bf16[2,1,2048,128]{3,2,1,0:T(8,128)(2,1)} %all-gather.3.cloned.1.call-done) | copy-start | bytes 3145732
  230.4 15.1 %all-to-all-start = ((f32[32,2,4,8]{3,2,1,0:T(4,128)}), f32[32,2,4,8]{3,2,1,0:T(4,128)S(1)}, u32[]{:S(2)}, u32[]{:S(2)}) async-start(f32[32,2,4,8]{3,2,1,0:T(4,128)} %bitcast.7), calls=%async_computation | async-start | bytes 262144 | tf_op jit(solution)/shard_map/all_to_all | solution.py:103
  245.5 16.9 %all-to-all-start.1 = ((bf16[32,2,4,1024]{3,2,1,0:T(4,128)(2,1)}), bf16[32,2,4,1024]{3,2,1,0:T(4,128)(2,1)S(1)}, u32[]{:S(2)}, u32[]{:S(2)}) async-start(bf16[32,2,4,1024]{3,2,1,0:T(4,128)(2,1)} %bitcast.14), calls=%async_computation.1 | async-start | bytes 1048576 | tf_op jit(solution)/shard_map/all_to_all | solution.py:100
  249.4 53.1 %reduce-scatter.2.cloned.1.call-start = ((), (), s32[]{:S(2)}) async-start(), calls=%async_computation.5 | async-start | bytes 589824 | tf_op jit(solution)/shard_map/reduce_scatter | solution.py:125
Sparse Core Ops, SparseCore 0:
  10.6 75.5 all-gather.2
  88.8 81.1 all-gather.4
  270.2 32.1 reduce-scatter.1
where the time goes:
time: 311 us; the launch traced here: 309 us
  waiting for transfers between devices  188 us (60%)
  matrix products  50.3 us (16%)
  other arithmetic  28 us (9%)
  local copies, waits for them, and re-layouts  18.5 us (6%)
  between operations  14 us (5%)
  starting transfers between devices  10 us (3%)
    all_gather x1, waiting for transfers between devices, on_device(): every_query = lax.all_gather(queries, 'ctx', axis=1, tiled=True)  80 us
    all_gather x1, waiting for transfers between devices, on_device(): span_all = lax.all_gather(span_kv, 'ctx', axis=2, tiled=True)  60.3 us
    reduce_scatter x1, waiting for transfers between devices, on_device(): lax.psum_scatter(jnp.dot(attended, out_weight, preferred_element_type=jnp...  31.6 us
    dot_general x3, matrix products, block_attention(): jnp.dot(weights, value_rows, preferred_element_type=jnp.float32) / totals  20.3 us
    reduce_sum x3, other arithmetic, block_attention(): totals = jnp.sum(exponent, axis=1, keepdims=True)  20.1 us
    dot_general x3, matrix products, block_attention(): lax.dot_general(query_rows, key_rows, (((1,), (1,)), ((), ())), preferred...  20 us
    all_to_all x1, waiting for transfers between devices, on_device(): lax.all_to_all(jnp.moveaxis(block_outs, 0, 1), 'ctx', split_axis=0, conca...  8.15 us
    all_to_all x1, waiting for transfers between devices, on_device(): lax.all_to_all(jnp.moveaxis(block_lses, 0, 1), 'ctx', split_axis=0, conca...  6.46 us
  transfers between devices with their start and end apart: 5, of which 5 were waited for; matrix products, arithmetic and copies ran while one was open for 9% of the time, Pallas kernels for 0%

commit v1 on v0

v1 whole, which is shorter than its diff:
```python
import functools
import math

import jax
import jax.numpy as jnp
from jax import lax
from jax.experimental import pallas as pl
from jax.experimental.pallas import tpu as pltpu
from jax.sharding import PartitionSpec as P

MESH = pl.DeviceIdType.MESH
F32 = jnp.float32
BF16 = jnp.bfloat16

NZ, NX, NK = 8, 4, 8
N = NZ * NX
QD = 64
HD = 128
GR = 8
TOP = 3
MOST = 4
NB = 64
BL = 4096
JB = 2
COLS = 4096
TILES = 4
PT = N // TILES
RT = PT * GR * MOST
SCALE = 1.0 / math.sqrt(HD)
EXP2 = SCALE * math.log2(math.e)
NT = (((1,), (1,)), ((), ()))


def iota(shape, dim):
    return lax.broadcasted_iota(jnp.int32, shape, dim)


def dot(a, b):
    return jnp.dot(a, b, preferred_element_type=F32)


def dot_nt(a, b):
    return lax.dot_general(a, b, NT, preferred_element_type=F32)


def offset_of(p):
    group, half, dx = lax.div(p, 8), lax.rem(lax.div(p, 4), 2), lax.rem(p, 4)
    return NZ + half * (2 * group + 1) - group, dx


def offset_vec(p):
    group, half, dx = p >> 3, (p >> 2) & 1, p & 3
    return NZ + half * (2 * group + 1) - group, dx


def one_hots(z, x, home, shape, dim):
    n = iota(shape, dim)
    dz, dx = offset_vec(n >> 4)
    dest = (((z + dz) & (NZ - 1)) << 2) | ((x + dx) & (NX - 1))
    return [(home == dest * JB + j).astype(BF16) for j in range(JB)]


def split3(v):
    hi = v.astype(BF16)
    rest = v - hi.astype(F32)
    mid = rest.astype(BF16)
    return hi, mid, (rest - mid.astype(F32)).astype(BF16)


def kernel(
    q_ref, span_ref, cache_ref, ch_ref, home_ref, w_ref, att_ref, proj_ref,
    kbuf, vbuf, wbuf, qsend, qrecv, osend, orecv, lsend, lrecv, sp, s_scr, p_scr, ret, own_o, own_l, rs_send, rs_recv,
    lsem, wsem, q_ss, q_rs, o_ss, o_rs, l_ss, l_rs, a_ss, a_rs, b_ss, b_rs, r_ss, r_rs,
):
    me = lax.axis_index("ctx")
    kv = lax.axis_index("kvh")
    z, x = lax.div(me, NX), lax.rem(me, NX)

    def peer(p, sign=1):
        dz, dx = offset_of(p)
        if sign < 0:
            dz, dx = 2 * NZ - dz, NX - dx
        return lax.rem(z + dz, NZ) * NX + lax.rem(x + dx, NX)

    loads = []
    for j in range(JB):
        rows = pl.ds(j * BL, BL)
        loads.append(pltpu.make_async_copy(cache_ref.at[0, 0, rows], kbuf.at[j], lsem.at[2 * j]))
        loads.append(pltpu.make_async_copy(cache_ref.at[1, 0, rows], vbuf.at[j], lsem.at[2 * j + 1]))
    w_load = pltpu.make_async_copy(w_ref, wbuf, wsem)
    for load in loads:
        load.start()
    w_load.start()

    barrier = pltpu.get_barrier_semaphore()

    @pl.loop(1, N)
    def _(p):
        pl.semaphore_signal(barrier, inc=1, device_id={"ctx": peer(p)}, device_id_type=MESH)

    @pl.loop(1, NK)
    def _(i):
        pl.semaphore_signal(barrier, inc=1, device_id={"kvh": lax.rem(kv + i, NK)}, device_id_type=MESH)

    width = 4 * QD
    lanes = iota((1, 128), 1)
    c4 = []
    for t in range(TOP):
        v = ch_ref[t, :, pl.ds(pl.multiple_of(lax.div(me, 2) * 128, 128), 128)]
        mine = jnp.where((lanes >> 6) == lax.rem(me, 2), v, jnp.concatenate([v[:, QD:], v[:, :QD]], axis=1))
        c4.append(jnp.concatenate([mine, mine], axis=1))
    chosen = functools.reduce(jnp.logical_or, [iota((NB, width), 0) == c for c in c4]).astype(BF16)
    home = home_ref[...]
    nrow = PT * TILES * 16
    places = one_hots(z, x, home, (nrow, 1), 0)
    r0, r1 = iota((width, width), 0), iota((width, width), 1)
    earlier = jnp.logical_and((r0 >> 6) == (r1 >> 6), r0 < r1).astype(BF16)
    rown = iota((nrow, width), 0)
    keep_gg = ((rown >> 2) & 3) == (iota((nrow, width), 1) >> 6)
    rank_n = (rown & 3).astype(F32)
    q = q_ref[0]
    stacked = [
        jnp.concatenate([q[:, (4 * gq + gg) * HD:(4 * gq + gg + 1) * HD] for gg in range(4)], axis=0)
        for gq in range(2)
    ]
    for j in range(JB):
        here = dot(places[j], chosen)
        rank = dot(here.astype(BF16), earlier)
        pick = jnp.where(jnp.logical_and(keep_gg, rank == rank_n), here, 0.0).astype(BF16)
        for gq in range(2):
            rows = dot(pick, stacked[gq]).astype(BF16).reshape(N, 16, HD)
            qsend[:, j, gq * 16:(gq + 1) * 16, :] = rows

    sp[x, :, pl.ds(pl.multiple_of(z * QD, QD), QD), :] = span_ref[:, 0]
    qrecv[0] = qsend[0]
    pl.semaphore_wait(barrier, N - 1 + NK - 1)

    @pl.loop(1, N)
    def _(p):
        pltpu.make_async_remote_copy(
            qsend.at[p], qrecv.at[p], q_ss, q_rs.at[lax.div(p, PT)], device_id={"ctx": peer(p)}, device_id_type=MESH
        ).start()

    mine_z = sp.at[x, :, pl.ds(pl.multiple_of(z * QD, QD), QD), :]

    @pl.loop(1, NZ)
    def _(i):
        pltpu.make_async_remote_copy(
            mine_z, mine_z, a_ss, a_rs, device_id={"ctx": lax.rem(z + i, NZ) * NX + x}, device_id_type=MESH
        ).start()

    c8 = jnp.concatenate(c4 + [jnp.zeros((8 - TOP, width), jnp.int32)], axis=0).astype(F32).T
    place_n = one_hots(z, x, home, (nrow, 1), 0)
    keep_t = (iota((width, nrow), 0) >> 6) == ((iota((width, nrow), 1) >> 2) & 3)
    rank_t = (iota((width, nrow), 1) & 3).astype(F32)
    later = jnp.logical_and((r0 >> 6) == (r1 >> 6), r1 < r0).astype(BF16)
    blocks = iota((width, NB), 1).astype(F32)
    one_t = [(c8[:, t:t + 1] == blocks).astype(BF16) for t in range(TOP)]
    any_t = one_t[0] + one_t[1] + one_t[2]
    f0, f1 = iota((nrow, 128), 0), iota((nrow, 128), 1)
    first_gg = ((f0 >> 2) & 3) == 0
    by_p = jnp.logical_and(first_gg, (f0 >> 4) == f1).astype(BF16)
    pick_p = [None] * TOP
    pick_jk = [None] * TOP
    for j in range(JB):
        rank = dot(later, dot_nt(any_t, place_n[j]).astype(BF16))
        keep = jnp.logical_and(keep_t, rank == rank_t)
        to_lane = jnp.logical_and(
            jnp.logical_and(first_gg, (f1 >> 5) == j), (f0 & 3) == (f1 & 3)
        ).astype(BF16)
        for t in range(TOP):
            pick = jnp.where(keep, dot_nt(one_t[t], place_n[j]), 0.0).astype(BF16)
            for gg in range(4):
                ret[j, pl.ds((gg * TOP + t) * QD, QD), :] = pick[gg * QD:(gg + 1) * QD]
            part_p, part_jk = dot(pick[:QD], by_p), dot(pick[:QD], to_lane)
            pick_p[t] = part_p if j == 0 else pick_p[t] + part_p
            pick_jk[t] = part_jk if j == 0 else pick_jk[t] + part_jk
    pick_p = jnp.concatenate(pick_p, axis=0).astype(BF16)
    pick_jk = jnp.concatenate(pick_jk, axis=0)
    own_l[1, 0:TOP * QD, :] = pick_jk
    own_l[1, TOP * QD:2 * TOP * QD, :] = pick_p.astype(F32)

    ones = jnp.ones((BL, HD), BF16)

    def softmax_rows(slot, keys, scores_of, values):
        peak = None
        step = 512
        for c in range(keys // step):
            s = scores_of(c)
            s_scr[slot, :, c * step:(c + 1) * step] = s
            for i in range(step // 128):
                piece = s[:, i * 128:(i + 1) * 128]
                peak = piece if peak is None else jnp.maximum(peak, piece)
        peak = jnp.max(peak, axis=1, keepdims=True)
        for c in range(keys // step):
            cols = slice(c * step, (c + 1) * step)
            p_scr[slot, :, cols] = jnp.exp2((s_scr[slot, :, cols] - peak) * EXP2).astype(BF16)
        acc = dot(p_scr[slot, :, :keys], jnp.concatenate([values, ones[:keys]], axis=1))
        total = acc[:, HD:]
        return acc[:, :HD] / total, peak * SCALE + jnp.log(total)

    for load in loads:
        load.wait()

    lane_of = iota((RT, 128), 1)
    row_in = iota((RT, 128), 0) & 31

    @pl.loop(0, TILES)
    def _(tile):
        @pl.when(tile == 0)
        def _():
            part = qrecv.at[pl.ds(0, PT - 1)]
            pltpu.make_async_copy(part, part, q_rs.at[0]).wait()

        @pl.when(tile > 0)
        def _():
            part = qrecv.at[pl.ds(0, PT)]
            pltpu.make_async_copy(part, part, q_rs.at[tile]).wait()

        @pl.when(tile == 1)
        def _():
            part = sp.at[0, :, pl.ds(0, (NZ - 1) * QD), :]
            pltpu.make_async_copy(part, part, a_rs).wait()

            @pl.loop(1, NX)
            def _(i):
                pltpu.make_async_remote_copy(
                    sp.at[x], sp.at[x], b_ss, b_rs, device_id={"ctx": z * NX + lax.rem(x + i, NX)}, device_id_type=MESH
                ).start()

        base = tile * PT
        lse_rows = jnp.zeros((PT, 128), F32)
        for j in range(JB):
            rows = qrecv[pl.ds(base, PT), j].reshape(RT, HD)
            out, lse = softmax_rows(
                j, BL, lambda c: dot_nt(rows, kbuf[j, c * 512:(c + 1) * 512, :]), vbuf[j]
            )
            osend[pl.ds(base, PT), j] = out.astype(BF16).reshape(PT, 32, HD)
            lse = jnp.where(lane_of == row_in + j * 32, lse, 0.0)
            lse_rows += jnp.sum(lse.reshape(PT, 32, 128), axis=1)
        lsend[pl.ds(base, PT)] = lse_rows.reshape(PT, 1, 128)

        @pl.loop(0, PT)
        def _(i):
            p = base + i

            @pl.when(p > 0)
            def _():
                who = {"ctx": peer(p, -1)}
                pltpu.make_async_remote_copy(
                    osend.at[p], orecv.at[p], o_ss, o_rs, device_id=who, device_id_type=MESH
                ).start()
                pltpu.make_async_remote_copy(
                    lsend.at[p], lrecv.at[p], l_ss, l_rs, device_id=who, device_id_type=MESH
                ).start()

    orecv[0] = osend[0]
    lrecv[0] = lsend[0]

    part = sp.at[pl.ds(0, NX - 1)]
    pltpu.make_async_copy(part, part, b_rs).wait()
    for half in range(2):
        rows = jnp.concatenate([q_ref[0, :, (4 * half + i) * HD:(4 * half + i + 1) * HD] for i in range(4)], axis=0)
        row_pos = me * QD + (iota((RT, 512), 0) & (QD - 1))
        col = iota((RT, 512), 1)

        def own_scores(c):
            key_pos = (col >> 6) * (NX * QD) + c * QD + (col & (QD - 1))
            return jnp.where(key_pos <= row_pos, dot_nt(rows, sp[c, 0]), -1e30)

        values = jnp.concatenate([sp[c, 1] for c in range(NX)], axis=0)
        out, lse = softmax_rows(half, NX * 512, own_scores, values)
        own_o[half * RT:(half + 1) * RT, :] = out
        own_l[0, half * RT:(half + 1) * RT, :] = lse

    part = orecv.at[pl.ds(0, N - 1)]
    pltpu.make_async_copy(part, part, o_rs).wait()
    part = lrecv.at[pl.ds(0, N - 1)]
    pltpu.make_async_copy(part, part, l_rs).wait()

    pick_jk = own_l[1, 0:TOP * QD, :]
    pick_p = own_l[1, TOP * QD:2 * TOP * QD, 0:N].astype(BF16)
    pieces = jnp.concatenate(split3(lrecv[...].reshape(N, 128)), axis=1)
    picked = dot(pick_p, pieces)
    picked = jnp.concatenate([picked[:, i * 128:(i + 1) * 128] * pick_jk for i in range(3)], axis=1).astype(BF16)
    e0, e1 = iota((3 * 128, GR * HD), 0) & 127, iota((3 * 128, GR * HD), 1)
    spread = jnp.logical_and(e0 < 64, ((e0 >> 2) & 7) == (e1 >> 7)).astype(BF16)
    far_lse = dot(picked, spread)
    for gq in range(2):
        parts = sum(dot(ret[j], orecv[:, j, gq * 16:(gq + 1) * 16, :].reshape(nrow, HD)) for j in range(JB))
        for gg in range(4):
            g = gq * 4 + gg
            lses = [own_l[0, g * QD:(g + 1) * QD, :]]
            outs = [own_o[g * QD:(g + 1) * QD, :]]
            for t in range(TOP):
                lses.append(far_lse[t * QD:(t + 1) * QD, g * HD:(g + 1) * HD])
                outs.append(parts[(gg * TOP + t) * QD:(gg * TOP + t + 1) * QD])
            peak = functools.reduce(jnp.maximum, lses)
            factors = [jnp.exp(v - peak) for v in lses]
            mixed = sum(f * o for f, o in zip(factors, outs)) / sum(factors)
            att_ref[0, :, g * HD:(g + 1) * HD] = mixed.astype(BF16)

    w_load.wait()
    att = att_ref[0]
    half = COLS // 2
    step = 512
    for c in range(half // step):
        left = dot(att, wbuf[:, c * step:(c + 1) * step])
        right = dot(att, wbuf[:, half + c * step:half + (c + 1) * step])
        for k in range(NK):
            both = jnp.concatenate([left[k * 8:(k + 1) * 8], right[k * 8:(k + 1) * 8]], axis=0)
            rs_send[k, :, c * step:(c + 1) * step] = both.astype(BF16)

    @pl.loop(1, NK)
    def _(i):
        dst = lax.rem(kv + i, NK)
        pltpu.make_async_remote_copy(
            rs_send.at[dst], rs_recv.at[i], r_ss, r_rs, device_id={"kvh": dst}, device_id_type=MESH
        ).start()

    part = rs_recv.at[pl.ds(0, NK - 1)]
    pltpu.make_async_copy(part, part, r_rs).wait()
    total = rs_send[kv].astype(F32)
    for i in range(1, NK):
        total += rs_recv[i].astype(F32)
    proj_ref[:, :half] = total[:8].astype(BF16)
    proj_ref[:, half:] = total[8:].astype(BF16)

    for buf, sem in ((qsend, q_ss), (osend, o_ss), (lsend, l_ss)):
        part = buf.at[pl.ds(0, N - 1)]
        pltpu.make_async_copy(part, part, sem).wait()
    part = sp.at[0, :, pl.ds(0, (NZ - 1) * QD), :]
    pltpu.make_async_copy(part, part, a_ss).wait()
    part = sp.at[pl.ds(0, NX - 1)]
    pltpu.make_async_copy(part, part, b_ss).wait()
    part = rs_send.at[pl.ds(0, NK - 1)]
    pltpu.make_async_copy(part, part, r_ss).wait()


def on_device(queries, span_kv, cache_kv, choices, block_home, out_weight):
    vmem = pl.BlockSpec(memory_space=pltpu.VMEM)
    hbm = pl.BlockSpec(memory_space=pl.ANY)
    dma = pltpu.SemaphoreType.DMA
    attended, projected = pl.pallas_call(
        kernel,
        out_shape=(
            jax.ShapeDtypeStruct((1, QD, GR * HD), BF16),
            jax.ShapeDtypeStruct((8, COLS), BF16),
        ),
        in_specs=[vmem, vmem, hbm, vmem, vmem, hbm],
        out_specs=(vmem, vmem),
        scratch_shapes=[
            pltpu.VMEM((JB, BL, HD), BF16),
            pltpu.VMEM((JB, BL, HD), BF16),
            pltpu.VMEM((GR * HD, COLS), BF16),
            pltpu.VMEM((N, JB, 32, HD), BF16),
            pltpu.VMEM((N, JB, 32, HD), BF16),
            pltpu.VMEM((N, JB, 32, HD), BF16),
            pltpu.VMEM((N, JB, 32, HD), BF16),
            pltpu.VMEM((N, 1, 128), F32),
            pltpu.VMEM((N, 1, 128), F32),
            pltpu.VMEM((NX, 2, NZ * QD, HD), BF16),
            pltpu.VMEM((JB, RT, BL), F32),
            pltpu.VMEM((JB, RT, BL), BF16),
            pltpu.VMEM((JB, 4 * TOP * QD, N * 16), BF16),
            pltpu.VMEM((GR * QD, HD), F32),
            pltpu.VMEM((2, GR * QD, HD), F32),
            pltpu.VMEM((NK, 16, COLS // 2), BF16),
            pltpu.VMEM((NK, 16, COLS // 2), BF16),
            dma((4,)),
            dma,
            dma,
            dma((TILES,)),
            dma, dma, dma, dma, dma, dma, dma, dma, dma, dma,
        ],
        compiler_params=pltpu.CompilerParams(
            collective_id=0, has_side_effects=True, vmem_limit_bytes=56 * 2**20
        ),
    )(
        queries,
        span_kv,
        cache_kv,
        jnp.transpose(choices, (2, 0, 1)),
        block_home.reshape(1, NB),
        out_weight,
    )
    return attended, projected


def solution(mesh):
    return jax.shard_map(
        on_device,
        mesh=mesh,
        in_specs=(
            P("kvh", "ctx", None),
            P(None, "kvh", "ctx", None),
            P(None, "kvh", "ctx", None),
            P("kvh", None, None),
            P(),
            P("kvh", None),
        ),
        out_specs=(P("kvh", "ctx", None), P(("ctx", "kvh"), None)),
        check_vma=False,
    )
```

time: 311 us -> 67.3 us (0.22)
  waiting for transfers between devices: 188 us -> 0 us
  Pallas kernels: 0 us -> 63.5 us
  matrix products: 50.3 us -> 0 us
  other arithmetic: 28 us -> 0 us
  local copies, waits for them, and re-layouts: 18.5 us -> 3.04 us
  between operations: 14 us -> 0.64 us
  starting transfers between devices: 10 us -> 0 us
    all_gather x2 -> x0, waiting for transfers between devices: 140 us -> none  [the longest x1 80 us: on_device(): every_query = lax.all_gather(queries, 'ctx', axis=1, tiled=True)]
    pallas_call x0 -> x1, Pallas kernels: none -> 63.5 us  [on_device(): pl.pallas_call(kernel, out_shape=(jax.ShapeDtypeStruct((1, QD, GR * HD),...]
    dot_general x8 -> x0, matrix products: 50.3 us -> none  [the longest x3 20.3 us: block_attention(): jnp.dot(weights, value_rows, preferred_element_type=jnp.float32) / totals]
    reduce_scatter x1 -> x0, waiting for transfers between devices: 31.6 us -> none  [on_device(): lax.psum_scatter(jnp.dot(attended, out_weight, preferred_element_type=jnp...]
    reduce_sum x9 -> x0, other arithmetic: 24.4 us -> none  [the longest x3 20.1 us: block_attention(): totals = jnp.sum(exponent, axis=1, keepdims=True)]
    all_to_all x2 -> x0, waiting for transfers between devices: 14.6 us -> none  [the longest x1 8.15 us: on_device(): lax.all_to_all(jnp.moveaxis(block_outs, 0, 1), 'ctx', split_axis=0, conca...]
    all_to_all x2 -> x0, starting transfers between devices: 9.67 us -> none  [the longest x1 5.78 us: on_device(): lax.all_to_all(jnp.moveaxis(block_lses, 0, 1), 'ctx', split_axis=0, conca...]
    slice x1 -> x0, local copies, waits for them, and re-layouts: 3.82 us -> none  [on_device(): cache_values = cache_kv[1, 0].reshape(blk_dev, block_len, head_dim)]
  transfers between devices with their start and end apart: 5 -> 0, of which waited for: 5 -> 0; matrix products, arithmetic and copies ran while one was open for 9% -> 0% of each run, Pallas kernels for 0% -> 0%
where the time goes in v1:
time: 67.3 us; the launch traced here: 67.2 us
  Pallas kernels  63.5 us (94%)
  local copies, waits for them, and re-layouts  3.04 us (5%)
    pallas_call x1, Pallas kernels, on_device(): pl.pallas_call(kernel, out_shape=(jax.ShapeDtypeStruct((1, QD, GR * HD),...  63.5 us
    unnamed x2, local copies, waits for them, and re-layouts  3.04 us

profile of v1, /device:TPU:1, one launch (start us, length us, event | category | flops | bytes accessed | tf_op | source)
XLA Modules:
  0.0 67.2 jit_solution(3802203040777677560)
XLA Ops:
  0.6 63.5 %shard_map.77 = (bf16[1,64,1024]{2,1,0:T(8,128)(2,1)}, bf16[8,4096]{1,0:T(8,128)(2,1)}) custom-call(bf16[1,64,1024]{2,1,0:T(8,128)(2,1)} %q_ref.1, bf16[2,1,64,128]{3,2,1,0:T(8,128)(2,1)} %span_ref.1, bf16[2,1,8192,128]{3,2,1,0:T(8,128)(2,1)} %cache_ref.1, s32[3,1,2048]{2,1,0:T(1,128)} %bitcast.2, s32[1,64]{1,0:T(1,128)} %bitcast.3, bf16[1024,4096]{1,0:T(8,128)(2,1)} %w_ref.1), custom_call_target="tpu_custom_call" | custom-call | tf_op jit(solution)/shard_map/pallas_call | solution.py:344
  64.1 1.6 %copy.10 = bf16[1,64,1024]{2,1,0:T(8,128)(2,1)} copy(bf16[1,64,1024]{2,1,0:T(8,128)(2,1)} %get-tuple-element.4) | data formatting | bytes 262144
  65.7 1.5 %copy.11 = bf16[8,4096]{1,0:T(8,128)(2,1)} copy(bf16[8,4096]{1,0:T(8,128)(2,1)} %get-tuple-element.5) | data formatting | bytes 131072

commit v2 on v1

--- a/solution.py
+++ b/solution.py
@@ -12,7 +12,7 @@
 F32 = jnp.float32
 BF16 = jnp.bfloat16
 
-NZ, NX, NK = 8, 4, 8
+NZ, NX, NY = 8, 4, 4
 N = NZ * NX
 QD = 64
 HD = 128
@@ -23,6 +23,8 @@
 BL = 4096
 JB = 2
 COLS = 4096
+CHUNKS = 4
+CW = COLS // CHUNKS
 TILES = 4
 PT = N // TILES
 RT = PT * GR * MOST
@@ -44,13 +46,13 @@
 
 
 def offset_of(p):
-    group, half, dx = lax.div(p, 8), lax.rem(lax.div(p, 4), 2), lax.rem(p, 4)
-    return NZ + half * (2 * group + 1) - group, dx
+    dx, i = lax.div(p, NZ), lax.rem(p, NZ)
+    return NZ + (2 * lax.rem(i, 2) - 1) * lax.div(i + 1, 2), dx
 
 
 def offset_vec(p):
-    group, half, dx = p >> 3, (p >> 2) & 1, p & 3
-    return NZ + half * (2 * group + 1) - group, dx
+    dx, i = p >> 3, p & 7
+    return NZ + (2 * (i & 1) - 1) * ((i + 1) >> 1), dx
 
 
 def one_hots(z, x, home, shape, dim):
@@ -60,6 +62,14 @@
     return [(home == dest * JB + j).astype(BF16) for j in range(JB)]
 
 
+def send(src, dst, ss, rs, who):
+    pltpu.make_async_remote_copy(src, dst, ss, rs, device_id=who, device_id_type=MESH).start()
+
+
+def wait_for(part, sem):
+    pltpu.make_async_copy(part, part, sem).wait()
+
+
 def split3(v):
     hi = v.astype(BF16)
     rest = v - hi.astype(F32)
@@ -68,9 +78,9 @@
 
 
 def kernel(
-    q_ref, span_ref, cache_ref, ch_ref, home_ref, w_ref, att_ref, proj_ref,
-    kbuf, vbuf, wbuf, qsend, qrecv, osend, orecv, lsend, lrecv, sp, s_scr, p_scr, ret, own_o, own_l, rs_send, rs_recv,
-    lsem, wsem, q_ss, q_rs, o_ss, o_rs, l_ss, l_rs, a_ss, a_rs, b_ss, b_rs, r_ss, r_rs,
+    q_hbm, span_ref, cache_ref, ch_hbm, home_hbm, w_ref, att_ref, proj_ref,
+    q_ref, ch_ref, home_ref, kbuf, vbuf, wbuf, qsend, qrecv, osend, orecv, lsend, lrecv, sp, s_scr, p_scr, ret, own_o, own_l, r_stage, r_recv, y_send, y_recv,
+    isem, lsem, wsem, q_ss, q_rs, o_ss, o_rs, l_ss, l_rs, a_ss, a_rs, b_ss, b_rs, r_ss, r_rs, y_ss, y_rs,
 ):
     me = lax.axis_index("ctx")
     kv = lax.axis_index("kvh")
@@ -82,6 +92,16 @@
             dz, dx = 2 * NZ - dz, NX - dx
         return lax.rem(z + dz, NZ) * NX + lax.rem(x + dx, NX)
 
+    mine_z = sp.at[x, :, pl.ds(pl.multiple_of(z * QD, QD), QD), :]
+    pair = pl.ds(pl.multiple_of(lax.div(me, 2) * 128, 128), 128)
+    inputs = [
+        pltpu.make_async_copy(span_ref.at[:, 0], mine_z, isem.at[0]),
+        pltpu.make_async_copy(ch_hbm.at[:, :, pair], ch_ref, isem.at[1]),
+        pltpu.make_async_copy(home_hbm, home_ref, isem.at[2]),
+        pltpu.make_async_copy(q_hbm, q_ref, isem.at[3]),
+    ]
+    for load in inputs:
+        load.start()
     loads = []
     for j in range(JB):
         rows = pl.ds(j * BL, BL)
@@ -98,15 +118,32 @@
     def _(p):
         pl.semaphore_signal(barrier, inc=1, device_id={"ctx": peer(p)}, device_id_type=MESH)
 
-    @pl.loop(1, NK)
+    core, y = lax.rem(kv, 2), lax.div(kv, 2)
+    sibling = {"kvh": kv + 1 - 2 * core}
+
+    def along_y(i):
+        return lax.rem(y + i, NY)
+
+    pl.semaphore_signal(barrier, inc=1, device_id=sibling, device_id_type=MESH)
+
+    @pl.loop(1, NY)
     def _(i):
-        pl.semaphore_signal(barrier, inc=1, device_id={"kvh": lax.rem(kv + i, NK)}, device_id_type=MESH)
-
+        pl.semaphore_signal(barrier, inc=1, device_id={"kvh": 2 * along_y(i) + core}, device_id_type=MESH)
+
+    inputs[0].wait()
+    pl.semaphore_wait(barrier, N - 1 + 1 + NY - 1)
+
+    @pl.loop(1, NZ)
+    def _(i):
+        send(mine_z, mine_z, a_ss, a_rs, {"ctx": lax.rem(z + i, NZ) * NX + x})
+
+    for load in inputs[1:]:
+        load.wait()
     width = 4 * QD
     lanes = iota((1, 128), 1)
     c4 = []
     for t in range(TOP):
-        v = ch_ref[t, :, pl.ds(pl.multiple_of(lax.div(me, 2) * 128, 128), 128)]
+        v = ch_ref[t]
         mine = jnp.where((lanes >> 6) == lax.rem(me, 2), v, jnp.concatenate([v[:, QD:], v[:, :QD]], axis=1))
         c4.append(jnp.concatenate([mine, mine], axis=1))
     chosen = functools.reduce(jnp.logical_or, [iota((NB, width), 0) == c for c in c4]).astype(BF16)
@@ -131,23 +168,11 @@
             rows = dot(pick, stacked[gq]).astype(BF16).reshape(N, 16, HD)
             qsend[:, j, gq * 16:(gq + 1) * 16, :] = rows
 
-    sp[x, :, pl.ds(pl.multiple_of(z * QD, QD), QD), :] = span_ref[:, 0]
     qrecv[0] = qsend[0]
-    pl.semaphore_wait(barrier, N - 1 + NK - 1)
 
     @pl.loop(1, N)
     def _(p):
-        pltpu.make_async_remote_copy(
-            qsend.at[p], qrecv.at[p], q_ss, q_rs.at[lax.div(p, PT)], device_id={"ctx": peer(p)}, device_id_type=MESH
-        ).start()
-
-    mine_z = sp.at[x, :, pl.ds(pl.multiple_of(z * QD, QD), QD), :]
-
-    @pl.loop(1, NZ)
-    def _(i):
-        pltpu.make_async_remote_copy(
-            mine_z, mine_z, a_ss, a_rs, device_id={"ctx": lax.rem(z + i, NZ) * NX + x}, device_id_type=MESH
-        ).start()
+        send(qsend.at[p], qrecv.at[p], q_ss, q_rs.at[lax.div(p, PT)], {"ctx": peer(p)})
 
     c8 = jnp.concatenate(c4 + [jnp.zeros((8 - TOP, width), jnp.int32)], axis=0).astype(F32).T
     place_n = one_hots(z, x, home, (nrow, 1), 0)
@@ -202,6 +227,13 @@
     for load in loads:
         load.wait()
 
+    part = sp.at[0, :, pl.ds(0, (NZ - 1) * QD), :]
+    wait_for(part, a_rs)
+
+    @pl.loop(1, NX)
+    def _(i):
+        send(sp.at[x], sp.at[x], b_ss, b_rs, {"ctx": z * NX + lax.rem(x + i, NX)})
+
     lane_of = iota((RT, 128), 1)
     row_in = iota((RT, 128), 0) & 31
 
@@ -210,23 +242,12 @@
         @pl.when(tile == 0)
         def _():
             part = qrecv.at[pl.ds(0, PT - 1)]
-            pltpu.make_async_copy(part, part, q_rs.at[0]).wait()
+            wait_for(part, q_rs.at[0])
 
         @pl.when(tile > 0)
         def _():
             part = qrecv.at[pl.ds(0, PT)]
-            pltpu.make_async_copy(part, part, q_rs.at[tile]).wait()
-
-        @pl.when(tile == 1)
-        def _():
-            part = sp.at[0, :, pl.ds(0, (NZ - 1) * QD), :]
-            pltpu.make_async_copy(part, part, a_rs).wait()
-
-            @pl.loop(1, NX)
-            def _(i):
-                pltpu.make_async_remote_copy(
-                    sp.at[x], sp.at[x], b_ss, b_rs, device_id={"ctx": z * NX + lax.rem(x + i, NX)}, device_id_type=MESH
-                ).start()
+            wait_for(part, q_rs.at[tile])
 
         base = tile * PT
         lse_rows = jnp.zeros((PT, 128), F32)
@@ -247,18 +268,14 @@
             @pl.when(p > 0)
             def _():
                 who = {"ctx": peer(p, -1)}
-                pltpu.make_async_remote_copy(
-                    osend.at[p], orecv.at[p], o_ss, o_rs, device_id=who, device_id_type=MESH
-                ).start()
-                pltpu.make_async_remote_copy(
-                    lsend.at[p], lrecv.at[p], l_ss, l_rs, device_id=who, device_id_type=MESH
-                ).start()
+                send(osend.at[p], orecv.at[p], o_ss, o_rs, who)
+                send(lsend.at[p], lrecv.at[p], l_ss, l_rs, who)
 
     orecv[0] = osend[0]
     lrecv[0] = lsend[0]
 
     part = sp.at[pl.ds(0, NX - 1)]
-    pltpu.make_async_copy(part, part, b_rs).wait()
+    wait_for(part, b_rs)
     for half in range(2):
         rows = jnp.concatenate([q_ref[0, :, (4 * half + i) * HD:(4 * half + i + 1) * HD] for i in range(4)], axis=0)
         row_pos = me * QD + (iota((RT, 512), 0) & (QD - 1))
@@ -274,9 +291,9 @@
         own_l[0, half * RT:(half + 1) * RT, :] = lse
 
     part = orecv.at[pl.ds(0, N - 1)]
-    pltpu.make_async_copy(part, part, o_rs).wait()
+    wait_for(part, o_rs)
     part = lrecv.at[pl.ds(0, N - 1)]
-    pltpu.make_async_copy(part, part, l_rs).wait()
+    wait_for(part, l_rs)
 
     pick_jk = own_l[1, 0:TOP * QD, :]
     pick_p = own_l[1, TOP * QD:2 * TOP * QD, 0:N].astype(BF16)
@@ -302,39 +319,44 @@
 
     w_load.wait()
     att = att_ref[0]
-    half = COLS // 2
-    step = 512
-    for c in range(half // step):
-        left = dot(att, wbuf[:, c * step:(c + 1) * step])
-        right = dot(att, wbuf[:, half + c * step:half + (c + 1) * step])
-        for k in range(NK):
-            both = jnp.concatenate([left[k * 8:(k + 1) * 8], right[k * 8:(k + 1) * 8]], axis=0)
-            rs_send[k, :, c * step:(c + 1) * step] = both.astype(BF16)
-
-    @pl.loop(1, NK)
-    def _(i):
-        dst = lax.rem(kv + i, NK)
-        pltpu.make_async_remote_copy(
-            rs_send.at[dst], rs_recv.at[i], r_ss, r_rs, device_id={"kvh": dst}, device_id_type=MESH
-        ).start()
-
-    part = rs_recv.at[pl.ds(0, NK - 1)]
-    pltpu.make_async_copy(part, part, r_rs).wait()
-    total = rs_send[kv].astype(F32)
-    for i in range(1, NK):
-        total += rs_recv[i].astype(F32)
-    proj_ref[:, :half] = total[:8].astype(BF16)
-    proj_ref[:, half:] = total[8:].astype(BF16)
+
+    def over_y(c):
+        wait_for(r_recv.at[c], r_rs.at[c])
+        both = r_stage[core, c].astype(F32) + r_recv[c].astype(F32)
+        y_send[c] = both.astype(BF16)
+
+        @pl.loop(1, NY)
+        def _(i):
+            to = along_y(i)
+            send(y_send.at[c, to], y_recv.at[c, i], y_ss, y_rs.at[c], {"kvh": 2 * to + core})
+
+    for c in range(CHUNKS):
+        part = dot(att, wbuf[:, c * CW:(c + 1) * CW])
+        for k in range(2 * NY):
+            rows = part[k * 8:(k + 1) * 8]
+            both = jnp.concatenate([rows[:, :CW // 2], rows[:, CW // 2:]], axis=0)
+            r_stage[k % 2, c, k // 2] = both.astype(BF16)
+        send(r_stage.at[1 - core, c], r_recv.at[c], r_ss, r_rs.at[c], sibling)
+        if c > 0:
+            over_y(c - 1)
+    over_y(CHUNKS - 1)
+    for c in range(CHUNKS):
+        wait_for(y_recv.at[c, pl.ds(1, NY - 1)], y_rs.at[c])
+        total = y_send[c, y].astype(F32)
+        for i in range(1, NY):
+            total += y_recv[c, i].astype(F32)
+        proj_ref[:, c * CW:c * CW + CW // 2] = total[:8].astype(BF16)
+        proj_ref[:, c * CW + CW // 2:(c + 1) * CW] = total[8:].astype(BF16)
 
     for buf, sem in ((qsend, q_ss), (osend, o_ss), (lsend, l_ss)):
         part = buf.at[pl.ds(0, N - 1)]
-        pltpu.make_async_copy(part, part, sem).wait()
+        wait_for(part, sem)
     part = sp.at[0, :, pl.ds(0, (NZ - 1) * QD), :]
-    pltpu.make_async_copy(part, part, a_ss).wait()
+    wait_for(part, a_ss)
     part = sp.at[pl.ds(0, NX - 1)]
-    pltpu.make_async_copy(part, part, b_ss).wait()
-    part = rs_send.at[pl.ds(0, NK - 1)]
-    pltpu.make_async_copy(part, part, r_ss).wait()
+    wait_for(part, b_ss)
+    wait_for(r_recv, r_ss)
+    wait_for(y_recv.at[:, pl.ds(1, NY - 1)], y_ss)
 
 
 def on_device(queries, span_kv, cache_kv, choices, block_home, out_weight):
@@ -344,12 +366,15 @@
     attended, projected = pl.pallas_call(
         kernel,
         out_shape=(
-            jax.ShapeDtypeStruct((1, QD, GR * HD), BF16),
-            jax.ShapeDtypeStruct((8, COLS), BF16),
+            pltpu.VMEM((1, QD, GR * HD), BF16),
+            pltpu.VMEM((8, COLS), BF16),
         ),
-        in_specs=[vmem, vmem, hbm, vmem, vmem, hbm],
+        in_specs=[hbm] * 6,
         out_specs=(vmem, vmem),
         scratch_shapes=[
+            pltpu.VMEM((1, QD, GR * HD), BF16),
+            pltpu.VMEM((TOP, 1, 128), jnp.int32),
+            pltpu.VMEM((1, NB), jnp.int32),
             pltpu.VMEM((JB, BL, HD), BF16),
             pltpu.VMEM((JB, BL, HD), BF16),
             pltpu.VMEM((GR * HD, COLS), BF16),
@@ -365,13 +390,20 @@
             pltpu.VMEM((JB, 4 * TOP * QD, N * 16), BF16),
             pltpu.VMEM((GR * QD, HD), F32),
             pltpu.VMEM((2, GR * QD, HD), F32),
-            pltpu.VMEM((NK, 16, COLS // 2), BF16),
-            pltpu.VMEM((NK, 16, COLS // 2), BF16),
+            pltpu.VMEM((2, CHUNKS, NY, 16, CW // 2), BF16),
+            pltpu.VMEM((CHUNKS, NY, 16, CW // 2), BF16),
+            pltpu.VMEM((CHUNKS, NY, 16, CW // 2), BF16),
+            pltpu.VMEM((CHUNKS, NY, 16, CW // 2), BF16),
+            dma((4,)),
             dma((4,)),
             dma,
             dma,
             dma((TILES,)),
-            dma, dma, dma, dma, dma, dma, dma, dma, dma, dma,
+            dma, dma, dma, dma, dma, dma, dma, dma,
+            dma,
+            dma((CHUNKS,)),
+            dma,
+            dma((CHUNKS,)),
         ],
         compiler_params=pltpu.CompilerParams(
             collective_id=0, has_side_effects=True, vmem_limit_bytes=56 * 2**20

time: 67.3 us -> 57.5 us (0.85)
  Pallas kernels: 63.5 us -> 55.5 us
  local copies, waits for them, and re-layouts: 3.04 us -> 1.29 us
    pallas_call x1, Pallas kernels: 63.5 us -> 55.5 us  [on_device(): pl.pallas_call(kernel, out_shape=(pltpu.VMEM((1, QD, GR * HD), BF16), plt...]
    unnamed x2, local copies, waits for them, and re-layouts: 3.04 us -> 1.29 us
where the time goes in v2:
time: 57.5 us; the launch traced here: 57.4 us
  Pallas kernels  55.5 us (97%)
  local copies, waits for them, and re-layouts  1.29 us (2%)
  between operations  0.64 us (1%)
    pallas_call x1, Pallas kernels, on_device(): pl.pallas_call(kernel, out_shape=(pltpu.VMEM((1, QD, GR * HD), BF16), plt...  55.5 us
    unnamed x2, local copies, waits for them, and re-layouts  1.29 us

profile of v2, /device:TPU:1, one launch (start us, length us, event | category | flops | bytes accessed | tf_op | source)
XLA Modules:
  0.0 57.4 jit_solution(11996821191336186745)
XLA Ops:
  0.6 55.5 %shard_map.77 = (bf16[1,64,1024]{2,1,0:T(8,128)(2,1)S(1)}, bf16[8,4096]{1,0:T(8,128)(2,1)S(1)}) custom-call(bf16[1,64,1024]{2,1,0:T(8,128)(2,1)} %q_hbm.1, bf16[2,1,64,128]{3,2,1,0:T(8,128)(2,1)} %span_ref.1, bf16[2,1,8192,128]{3,2,1,0:T(8,128)(2,1)} %cache_ref.1, s32[3,1,2048]{2,1,0:T(1,128)} %bitcast.2, s32[1,64]{1,0:T(1,128)} %bitcast.3, ...), custom_call_target="tpu_custom_call" | custom-call | tf_op jit(solution)/shard_map/pallas_call | solution.py:366
  56.1 0.7 %copy.10 = bf16[1,64,1024]{2,1,0:T(8,128)(2,1)} copy(bf16[1,64,1024]{2,1,0:T(8,128)(2,1)S(1)} %get-tuple-element.2) | data formatting | bytes 262144
  56.7 0.6 %copy.11 = bf16[8,4096]{1,0:T(8,128)(2,1)} copy(bf16[8,4096]{1,0:T(8,128)(2,1)S(1)} %get-tuple-element.3) | data formatting | bytes 131072

commit v3 on v2

--- a/solution.py
+++ b/solution.py
@@ -79,8 +79,8 @@
 
 def kernel(
     q_hbm, span_ref, cache_ref, ch_hbm, home_hbm, w_ref, att_ref, proj_ref,
-    q_ref, ch_ref, home_ref, kbuf, vbuf, wbuf, qsend, qrecv, osend, orecv, lsend, lrecv, sp, s_scr, p_scr, ret, own_o, own_l, r_stage, r_recv, y_send, y_recv,
-    isem, lsem, wsem, q_ss, q_rs, o_ss, o_rs, l_ss, l_rs, a_ss, a_rs, b_ss, b_rs, r_ss, r_rs, y_ss, y_rs,
+    q_ref, ch_ref, home_ref, kbuf, vbuf, wbuf, qsend, qrecv, osend, orecv, lsend, lrecv, sp, s_scr, p_scr, ret, own_o, own_l, weight, r_stage, r_recv, y_send, y_recv,
+    isem, lsem, wsem, q_ss, q_rs, o_ss, o_rs, l_ss, l_rs, a_ss, a_rs, a2_rs, b_ss, b_rs, r_ss, r_rs, y_ss, y_rs,
 ):
     me = lax.axis_index("ctx")
     kv = lax.axis_index("kvh")
@@ -91,6 +91,24 @@
         if sign < 0:
             dz, dx = 2 * NZ - dz, NX - dx
         return lax.rem(z + dz, NZ) * NX + lax.rem(x + dx, NX)
+
+    barrier = pltpu.get_barrier_semaphore()
+
+    @pl.loop(1, N)
+    def _(p):
+        pl.semaphore_signal(barrier, inc=1, device_id={"ctx": peer(p)}, device_id_type=MESH)
+
+    core, y = lax.rem(kv, 2), lax.div(kv, 2)
+    sibling = {"kvh": kv + 1 - 2 * core}
+
+    def along_y(i):
+        return lax.rem(y + i, NY)
+
+    pl.semaphore_signal(barrier, inc=1, device_id=sibling, device_id_type=MESH)
+
+    @pl.loop(1, NY)
+    def _(i):
+        pl.semaphore_signal(barrier, inc=1, device_id={"kvh": 2 * along_y(i) + core}, device_id_type=MESH)
 
     mine_z = sp.at[x, :, pl.ds(pl.multiple_of(z * QD, QD), QD), :]
     pair = pl.ds(pl.multiple_of(lax.div(me, 2) * 128, 128), 128)
@@ -112,30 +130,17 @@
         load.start()
     w_load.start()
 
-    barrier = pltpu.get_barrier_semaphore()
-
-    @pl.loop(1, N)
-    def _(p):
-        pl.semaphore_signal(barrier, inc=1, device_id={"ctx": peer(p)}, device_id_type=MESH)
-
-    core, y = lax.rem(kv, 2), lax.div(kv, 2)
-    sibling = {"kvh": kv + 1 - 2 * core}
-
-    def along_y(i):
-        return lax.rem(y + i, NY)
-
-    pl.semaphore_signal(barrier, inc=1, device_id=sibling, device_id_type=MESH)
-
-    @pl.loop(1, NY)
-    def _(i):
-        pl.semaphore_signal(barrier, inc=1, device_id={"kvh": 2 * along_y(i) + core}, device_id_type=MESH)
-
     inputs[0].wait()
     pl.semaphore_wait(barrier, N - 1 + 1 + NY - 1)
 
-    @pl.loop(1, NZ)
-    def _(i):
-        send(mine_z, mine_z, a_ss, a_rs, {"ctx": lax.rem(z + i, NZ) * NX + x})
+    def at_z(d):
+        return lax.rem(z + NZ + d, NZ)
+
+    def send_z(src, sem, d):
+        send(src, src, a_ss, sem, {"ctx": at_z(d) * NX + x})
+
+    for d in (1, -1, 2, -2):
+        send_z(mine_z, a_rs, d)
 
     for load in inputs[1:]:
         load.wait()
@@ -170,9 +175,20 @@
 
     qrecv[0] = qsend[0]
 
-    @pl.loop(1, N)
-    def _(p):
+    def send_rows(p):
         send(qsend.at[p], qrecv.at[p], q_ss, q_rs.at[lax.div(p, PT)], {"ctx": peer(p)})
+
+    pl.loop(1, PT)(send_rows)
+
+    wait_for(sp.at[0, :, pl.ds(0, 4 * QD), :], a_rs)
+    below = pl.ds(pl.multiple_of(at_z(-2) * QD, QD), QD)
+    above = pl.ds(pl.multiple_of(at_z(2) * QD, QD), QD)
+    send_z(sp.at[x, :, below], a2_rs, 1)
+    send_z(sp.at[x, :, above], a2_rs, -1)
+    send_z(sp.at[x, 0, below], a2_rs, 2)
+    send_z(sp.at[x, 1, above], a2_rs, -2)
+
+    pl.loop(PT, N)(send_rows)
 
     c8 = jnp.concatenate(c4 + [jnp.zeros((8 - TOP, width), jnp.int32)], axis=0).astype(F32).T
     place_n = one_hots(z, x, home, (nrow, 1), 0)
@@ -227,8 +243,7 @@
     for load in loads:
         load.wait()
 
-    part = sp.at[0, :, pl.ds(0, (NZ - 1) * QD), :]
-    wait_for(part, a_rs)
+    wait_for(sp.at[0, :, pl.ds(0, 3 * QD), :], a2_rs)
 
     @pl.loop(1, NX)
     def _(i):
@@ -251,25 +266,51 @@
 
         base = tile * PT
         lse_rows = jnp.zeros((PT, 128), F32)
-        for j in range(JB):
-            rows = qrecv[pl.ds(base, PT), j].reshape(RT, HD)
-            out, lse = softmax_rows(
-                j, BL, lambda c: dot_nt(rows, kbuf[j, c * 512:(c + 1) * 512, :]), vbuf[j]
-            )
-            osend[pl.ds(base, PT), j] = out.astype(BF16).reshape(PT, 32, HD)
-            lse = jnp.where(lane_of == row_in + j * 32, lse, 0.0)
-            lse_rows += jnp.sum(lse.reshape(PT, 32, 128), axis=1)
+        step = 512
+        rows = [qrecv[pl.ds(base, PT), j].reshape(RT, HD) for j in range(JB)]
+
+        def scores(j, c, peak):
+            s = dot_nt(rows[j], kbuf[j, c * step:(c + 1) * step, :])
+            s_scr[j, :, c * step:(c + 1) * step] = s
+            for i in range(step // 128):
+                piece = s[:, i * 128:(i + 1) * 128]
+                peak = piece if peak is None else jnp.maximum(peak, piece)
+            return peak
+
+        def weigh(j, c, peak, acc):
+            cols = slice(c * step, (c + 1) * step)
+            p = jnp.exp2((s_scr[j, :, cols] - peak) * EXP2).astype(BF16)
+            new = dot(p, jnp.concatenate([vbuf[j, cols], ones[cols]], axis=1))
+            return new if acc is None else acc + new
+
+        def finish(j, peak, acc):
+            total = acc[:, HD:]
+            osend[pl.ds(base, PT), j] = (acc[:, :HD] / total).astype(BF16).reshape(PT, 32, HD)
+            lse = jnp.where(lane_of == row_in + j * 32, peak * SCALE + jnp.log(total), 0.0)
+            return jnp.sum(lse.reshape(PT, 32, 128), axis=1)
+
+        peak0 = peak1 = acc0 = acc1 = None
+        for c in range(BL // step):
+            peak0 = scores(0, c, peak0)
+        peak0 = jnp.max(peak0, axis=1, keepdims=True)
+        for c in range(BL // step):
+            peak1 = scores(1, c, peak1)
+            acc0 = weigh(0, c, peak0, acc0)
+        peak1 = jnp.max(peak1, axis=1, keepdims=True)
+        for c in range(BL // step):
+            acc1 = weigh(1, c, peak1, acc1)
+        lse_rows = finish(0, peak0, acc0) + finish(1, peak1, acc1)
         lsend[pl.ds(base, PT)] = lse_rows.reshape(PT, 1, 128)
 
-        @pl.loop(0, PT)
-        def _(i):
+        def send_back(i, src, dst, ss, rs):
             p = base + i
 
             @pl.when(p > 0)
             def _():
-                who = {"ctx": peer(p, -1)}
-                send(osend.at[p], orecv.at[p], o_ss, o_rs, who)
-                send(lsend.at[p], lrecv.at[p], l_ss, l_rs, who)
+                send(src.at[p], dst.at[p], ss, rs, {"ctx": peer(p, -1)})
+
+        pl.loop(0, PT)(lambda i: send_back(i, lsend, lrecv, l_ss, l_rs))
+        pl.loop(0, PT)(lambda i: send_back(i, osend, orecv, o_ss, o_rs.at[tile]))
 
     orecv[0] = osend[0]
     lrecv[0] = lsend[0]
@@ -290,11 +331,7 @@
         own_o[half * RT:(half + 1) * RT, :] = out
         own_l[0, half * RT:(half + 1) * RT, :] = lse
 
-    part = orecv.at[pl.ds(0, N - 1)]
-    wait_for(part, o_rs)
-    part = lrecv.at[pl.ds(0, N - 1)]
-    wait_for(part, l_rs)
-
+    wait_for(lrecv.at[pl.ds(0, N - 1)], l_rs)
     pick_jk = own_l[1, 0:TOP * QD, :]
     pick_p = own_l[1, TOP * QD:2 * TOP * QD, 0:N].astype(BF16)
     pieces = jnp.concatenate(split3(lrecv[...].reshape(N, 128)), axis=1)
@@ -303,19 +340,33 @@
     e0, e1 = iota((3 * 128, GR * HD), 0) & 127, iota((3 * 128, GR * HD), 1)
     spread = jnp.logical_and(e0 < 64, ((e0 >> 2) & 7) == (e1 >> 7)).astype(BF16)
     far_lse = dot(picked, spread)
-    for gq in range(2):
-        parts = sum(dot(ret[j], orecv[:, j, gq * 16:(gq + 1) * 16, :].reshape(nrow, HD)) for j in range(JB))
-        for gg in range(4):
-            g = gq * 4 + gg
-            lses = [own_l[0, g * QD:(g + 1) * QD, :]]
-            outs = [own_o[g * QD:(g + 1) * QD, :]]
-            for t in range(TOP):
-                lses.append(far_lse[t * QD:(t + 1) * QD, g * HD:(g + 1) * HD])
-                outs.append(parts[(gg * TOP + t) * QD:(gg * TOP + t + 1) * QD])
-            peak = functools.reduce(jnp.maximum, lses)
-            factors = [jnp.exp(v - peak) for v in lses]
-            mixed = sum(f * o for f, o in zip(factors, outs)) / sum(factors)
-            att_ref[0, :, g * HD:(g + 1) * HD] = mixed.astype(BF16)
+    for g in range(GR):
+        rows = slice(g * QD, (g + 1) * QD)
+        lses = [own_l[0, rows, :]] + [far_lse[t * QD:(t + 1) * QD, g * HD:(g + 1) * HD] for t in range(TOP)]
+        peak = functools.reduce(jnp.maximum, lses)
+        factors = [jnp.exp(v - peak) for v in lses]
+        whole = sum(factors)
+        own_o[rows, :] = own_o[rows, :] * (factors[0] / whole)
+        for t in range(TOP):
+            weight[t, rows, :] = factors[t + 1] / whole
+
+    parts = [None, None]
+    for tile in range(TILES):
+        first = 1 if tile == 0 else 0
+        wait_for(orecv.at[pl.ds(first, PT - first)], o_rs.at[tile])
+        cols = slice(tile * PT * 16, (tile + 1) * PT * 16)
+        for gq in range(2):
+            for j in range(JB):
+                back = orecv[tile * PT:(tile + 1) * PT, j, gq * 16:(gq + 1) * 16, :].reshape(PT * 16, HD)
+                new = dot(ret[j, :, cols], back)
+                parts[gq] = new if parts[gq] is None else parts[gq] + new
+    for g in range(GR):
+        rows = slice(g * QD, (g + 1) * QD)
+        mixed = own_o[rows, :]
+        for t in range(TOP):
+            first = (g % 4 * TOP + t) * QD
+            mixed += weight[t, rows, :] * parts[g // 4][first:first + QD]
+        att_ref[0, :, g * HD:(g + 1) * HD] = mixed.astype(BF16)
 
     w_load.wait()
     att = att_ref[0]
@@ -390,6 +441,7 @@
             pltpu.VMEM((JB, 4 * TOP * QD, N * 16), BF16),
             pltpu.VMEM((GR * QD, HD), F32),
             pltpu.VMEM((2, GR * QD, HD), F32),
+            pltpu.VMEM((TOP, GR * QD, HD), F32),
             pltpu.VMEM((2, CHUNKS, NY, 16, CW // 2), BF16),
             pltpu.VMEM((CHUNKS, NY, 16, CW // 2), BF16),
             pltpu.VMEM((CHUNKS, NY, 16, CW // 2), BF16),
@@ -399,7 +451,9 @@
             dma,
             dma,
             dma((TILES,)),
-            dma, dma, dma, dma, dma, dma, dma, dma,
+            dma,
+            dma((TILES,)),
+            dma, dma, dma, dma, dma, dma, dma,
             dma,
             dma((CHUNKS,)),
             dma,

time: 57.5 us -> 54.1 us (0.941)
  Pallas kernels: 55.5 us -> 52.1 us
    pallas_call x1, Pallas kernels: 55.5 us -> 52.1 us  [on_device(): pl.pallas_call(kernel, out_shape=(pltpu.VMEM((1, QD, GR * HD), BF16), plt...]
where the time goes in v3:
time: 54.1 us; the launch traced here: 54 us
  Pallas kernels  52.1 us (96%)
  local copies, waits for them, and re-layouts  1.29 us (2%)
  between operations  0.64 us (1%)
    pallas_call x1, Pallas kernels, on_device(): pl.pallas_call(kernel, out_shape=(pltpu.VMEM((1, QD, GR * HD), BF16), plt...  52.1 us
    unnamed x2, local copies, waits for them, and re-layouts  1.29 us

profile of v3, /device:TPU:1, one launch (start us, length us, event | category | flops | bytes accessed | tf_op | source)
XLA Modules:
  0.0 54.0 jit_solution(16247047795736049400)
XLA Ops:
  0.6 52.1 %shard_map.77 = (bf16[1,64,1024]{2,1,0:T(8,128)(2,1)S(1)}, bf16[8,4096]{1,0:T(8,128)(2,1)S(1)}) custom-call(bf16[1,64,1024]{2,1,0:T(8,128)(2,1)} %q_hbm.1, bf16[2,1,64,128]{3,2,1,0:T(8,128)(2,1)} %span_ref.1, bf16[2,1,8192,128]{3,2,1,0:T(8,128)(2,1)} %cache_ref.1, s32[3,1,2048]{2,1,0:T(1,128)} %bitcast.2, s32[1,64]{1,0:T(1,128)} %bitcast.3, ...), custom_call_target="tpu_custom_call" | custom-call | tf_op jit(solution)/shard_map/pallas_call | solution.py:417
  52.8 0.7 %copy.10 = bf16[1,64,1024]{2,1,0:T(8,128)(2,1)} copy(bf16[1,64,1024]{2,1,0:T(8,128)(2,1)S(1)} %get-tuple-element.2) | data formatting | bytes 262144
  53.4 0.6 %copy.11 = bf16[8,4096]{1,0:T(8,128)(2,1)} copy(bf16[8,4096]{1,0:T(8,128)(2,1)S(1)} %get-tuple-element.3) | data formatting | bytes 131072

commit v4 on v3

--- a/solution.py
+++ b/solution.py
@@ -79,7 +79,7 @@
 
 def kernel(
     q_hbm, span_ref, cache_ref, ch_hbm, home_hbm, w_ref, att_ref, proj_ref,
-    q_ref, ch_ref, home_ref, kbuf, vbuf, wbuf, qsend, qrecv, osend, orecv, lsend, lrecv, sp, s_scr, p_scr, ret, own_o, own_l, weight, r_stage, r_recv, y_send, y_recv,
+    q_ref, ch_ref, home_ref, kbuf, vbuf, wbuf, qsend, qrecv, osend, orecv, lsend, lrecv, sp, s_scr, ret, own_o, own_l, weight, r_stage, r_recv, y_send, y_recv,
     isem, lsem, wsem, q_ss, q_rs, o_ss, o_rs, l_ss, l_rs, a_ss, a_rs, a2_rs, b_ss, b_rs, r_ss, r_rs, y_ss, y_rs,
 ):
     me = lax.axis_index("ctx")
@@ -139,8 +139,10 @@
     def send_z(src, sem, d):
         send(src, src, a_ss, sem, {"ctx": at_z(d) * NX + x})
 
-    for d in (1, -1, 2, -2):
+    for d in (2, -2):
         send_z(mine_z, a_rs, d)
+    for d in (1, -1):
+        send_z(mine_z, a2_rs, d)
 
     for load in inputs[1:]:
         load.wait()
@@ -180,7 +182,7 @@
 
     pl.loop(1, PT)(send_rows)
 
-    wait_for(sp.at[0, :, pl.ds(0, 4 * QD), :], a_rs)
+    wait_for(sp.at[0, :, pl.ds(0, 2 * QD), :], a_rs)
     below = pl.ds(pl.multiple_of(at_z(-2) * QD, QD), QD)
     above = pl.ds(pl.multiple_of(at_z(2) * QD, QD), QD)
     send_z(sp.at[x, :, below], a2_rs, 1)
@@ -223,31 +225,14 @@
 
     ones = jnp.ones((BL, HD), BF16)
 
-    def softmax_rows(slot, keys, scores_of, values):
-        peak = None
-        step = 512
-        for c in range(keys // step):
-            s = scores_of(c)
-            s_scr[slot, :, c * step:(c + 1) * step] = s
-            for i in range(step // 128):
-                piece = s[:, i * 128:(i + 1) * 128]
-                peak = piece if peak is None else jnp.maximum(peak, piece)
-        peak = jnp.max(peak, axis=1, keepdims=True)
-        for c in range(keys // step):
-            cols = slice(c * step, (c + 1) * step)
-            p_scr[slot, :, cols] = jnp.exp2((s_scr[slot, :, cols] - peak) * EXP2).astype(BF16)
-        acc = dot(p_scr[slot, :, :keys], jnp.concatenate([values, ones[:keys]], axis=1))
-        total = acc[:, HD:]
-        return acc[:, :HD] / total, peak * SCALE + jnp.log(total)
-
     for load in loads:
         load.wait()
 
-    wait_for(sp.at[0, :, pl.ds(0, 3 * QD), :], a2_rs)
+    wait_for(sp.at[0, :, pl.ds(0, 5 * QD), :], a2_rs)
 
     @pl.loop(1, NX)
     def _(i):
-        send(sp.at[x], sp.at[x], b_ss, b_rs, {"ctx": z * NX + lax.rem(x + i, NX)})
+        send(sp.at[x], sp.at[x], b_ss, b_rs.at[i], {"ctx": z * NX + lax.rem(x + i, NX)})
 
     lane_of = iota((RT, 128), 1)
     row_in = iota((RT, 128), 0) & 31
@@ -315,21 +300,44 @@
     orecv[0] = osend[0]
     lrecv[0] = lsend[0]
 
-    part = sp.at[pl.ds(0, NX - 1)]
-    wait_for(part, b_rs)
-    for half in range(2):
-        rows = jnp.concatenate([q_ref[0, :, (4 * half + i) * HD:(4 * half + i + 1) * HD] for i in range(4)], axis=0)
-        row_pos = me * QD + (iota((RT, 512), 0) & (QD - 1))
-        col = iota((RT, 512), 1)
-
-        def own_scores(c):
-            key_pos = (col >> 6) * (NX * QD) + c * QD + (col & (QD - 1))
-            return jnp.where(key_pos <= row_pos, dot_nt(rows, sp[c, 0]), -1e30)
-
-        values = jnp.concatenate([sp[c, 1] for c in range(NX)], axis=0)
-        out, lse = softmax_rows(half, NX * 512, own_scores, values)
-        own_o[half * RT:(half + 1) * RT, :] = out
-        own_l[0, half * RT:(half + 1) * RT, :] = lse
+    own_rows = [
+        jnp.concatenate([q_ref[0, :, (4 * h + i) * HD:(4 * h + i + 1) * HD] for i in range(4)], axis=0)
+        for h in range(2)
+    ]
+    step = NZ * QD
+    row_pos = me * QD + (iota((RT, step), 0) & (QD - 1))
+    col = iota((RT, step), 1)
+    key_pos = (col >> 6) * (NX * QD) + (col & (QD - 1))
+
+    xs = [lax.rem(x + NX - c, NX) for c in range(NX)]
+
+    def own_scores(h, c, peak):
+        s = jnp.where(key_pos + xs[c] * QD <= row_pos, dot_nt(own_rows[h], sp[xs[c], 0]), -1e30)
+        s_scr[h, :, c * step:(c + 1) * step] = s
+        for i in range(step // 128):
+            piece = s[:, i * 128:(i + 1) * 128]
+            peak = piece if peak is None else jnp.maximum(peak, piece)
+        return peak
+
+    def own_weigh(h, c, peak, acc):
+        p = jnp.exp2((s_scr[h, :, c * step:(c + 1) * step] - peak) * EXP2).astype(BF16)
+        new = dot(p, jnp.concatenate([sp[xs[c], 1], ones[:step]], axis=1))
+        return new if acc is None else acc + new
+
+    peaks, accs = [None, None], [None, None]
+    for c in range(NX):
+        if c > 0:
+            wait_for(sp.at[0], b_rs.at[c])
+        for h in range(2):
+            peaks[h] = own_scores(h, c, peaks[h])
+    for h in range(2):
+        peaks[h] = jnp.max(peaks[h], axis=1, keepdims=True)
+        for c in range(NX):
+            accs[h] = own_weigh(h, c, peaks[h], accs[h])
+    for h in range(2):
+        total = accs[h][:, HD:]
+        own_o[h * RT:(h + 1) * RT, :] = accs[h][:, :HD] / total
+        own_l[0, h * RT:(h + 1) * RT, :] = peaks[h] * SCALE + jnp.log(total)
 
     wait_for(lrecv.at[pl.ds(0, N - 1)], l_rs)
     pick_jk = own_l[1, 0:TOP * QD, :]
@@ -437,7 +445,6 @@
             pltpu.VMEM((N, 1, 128), F32),
             pltpu.VMEM((NX, 2, NZ * QD, HD), BF16),
             pltpu.VMEM((JB, RT, BL), F32),
-            pltpu.VMEM((JB, RT, BL), BF16),
             pltpu.VMEM((JB, 4 * TOP * QD, N * 16), BF16),
             pltpu.VMEM((GR * QD, HD), F32),
             pltpu.VMEM((2, GR * QD, HD), F32),
@@ -453,7 +460,8 @@
             dma((TILES,)),
             dma,
             dma((TILES,)),
-            dma, dma, dma, dma, dma, dma, dma,
+            dma, dma, dma, dma, dma, dma,
+            dma((NX,)),
             dma,
             dma((CHUNKS,)),
             dma,

time: 54.1 us -> 53.6 us (level)
  no operation moved by 1% of the time
where the time goes in v4:
time: 53.6 us
  Pallas kernels  51.6 us (96%)
  local copies, waits for them, and re-layouts  1.29 us (2%)
  between operations  0.64 us (1%)
    pallas_call x1, Pallas kernels, on_device(): pl.pallas_call(kernel, out_shape=(pltpu.VMEM((1, QD, GR * HD), BF16), plt...  51.6 us
    unnamed x2, local copies, waits for them, and re-layouts  1.29 us

profile of v4, /device:TPU:1, one launch (start us, length us, event | category | flops | bytes accessed | tf_op | source)
XLA Modules:
  0.0 53.6 jit_solution(7050305854106505007)
XLA Ops:
  0.6 51.6 %shard_map.77 = (bf16[1,64,1024]{2,1,0:T(8,128)(2,1)S(1)}, bf16[8,4096]{1,0:T(8,128)(2,1)S(1)}) custom-call(bf16[1,64,1024]{2,1,0:T(8,128)(2,1)} %q_hbm.1, bf16[2,1,64,128]{3,2,1,0:T(8,128)(2,1)} %span_ref.1, bf16[2,1,8192,128]{3,2,1,0:T(8,128)(2,1)} %cache_ref.1, s32[3,1,2048]{2,1,0:T(1,128)} %bitcast.2, s32[1,64]{1,0:T(1,128)} %bitcast.3, ...), custom_call_target="tpu_custom_call" | custom-call | tf_op jit(solution)/shard_map/pallas_call | solution.py:425
  52.3 0.7 %copy.10 = bf16[1,64,1024]{2,1,0:T(8,128)(2,1)} copy(bf16[1,64,1024]{2,1,0:T(8,128)(2,1)S(1)} %get-tuple-element.2) | data formatting | bytes 262144
  52.9 0.6 %copy.11 = bf16[8,4096]{1,0:T(8,128)(2,1)} copy(bf16[8,4096]{1,0:T(8,128)(2,1)S(1)} %get-tuple-element.3) | data formatting | bytes 131072

commit v5 on v4

--- a/solution.py
+++ b/solution.py
@@ -384,8 +384,7 @@
         both = r_stage[core, c].astype(F32) + r_recv[c].astype(F32)
         y_send[c] = both.astype(BF16)
 
-        @pl.loop(1, NY)
-        def _(i):
+        for i in (2, 1, 3):
             to = along_y(i)
             send(y_send.at[c, to], y_recv.at[c, i], y_ss, y_rs.at[c], {"kvh": 2 * to + core})
 

time: 53.6 us -> 53.4 us (level)
  no operation moved by 1% of the time
where the time goes in v5:
time: 53.4 us
  Pallas kernels  51.4 us (96%)
  local copies, waits for them, and re-layouts  1.29 us (2%)
  between operations  0.64 us (1%)
    pallas_call x1, Pallas kernels, on_device(): pl.pallas_call(kernel, out_shape=(pltpu.VMEM((1, QD, GR * HD), BF16), plt...  51.4 us
    unnamed x2, local copies, waits for them, and re-layouts  1.29 us

profile of v5, /device:TPU:1, one launch (start us, length us, event | category | flops | bytes accessed | tf_op | source)
XLA Modules:
  0.0 53.4 jit_solution(6945494215578107919)
XLA Ops:
  0.6 51.4 %shard_map.77 = (bf16[1,64,1024]{2,1,0:T(8,128)(2,1)S(1)}, bf16[8,4096]{1,0:T(8,128)(2,1)S(1)}) custom-call(bf16[1,64,1024]{2,1,0:T(8,128)(2,1)} %q_hbm.1, bf16[2,1,64,128]{3,2,1,0:T(8,128)(2,1)} %span_ref.1, bf16[2,1,8192,128]{3,2,1,0:T(8,128)(2,1)} %cache_ref.1, s32[3,1,2048]{2,1,0:T(1,128)} %bitcast.2, s32[1,64]{1,0:T(1,128)} %bitcast.3, ...), custom_call_target="tpu_custom_call" | custom-call | tf_op jit(solution)/shard_map/pallas_call | solution.py:424
  52.1 0.7 %copy.10 = bf16[1,64,1024]{2,1,0:T(8,128)(2,1)} copy(bf16[1,64,1024]{2,1,0:T(8,128)(2,1)S(1)} %get-tuple-element.2) | data formatting | bytes 262144
  52.7 0.6 %copy.11 = bf16[8,4096]{1,0:T(8,128)(2,1)} copy(bf16[8,4096]{1,0:T(8,128)(2,1)S(1)} %get-tuple-element.3) | data formatting | bytes 131072
